TPU v7x, 512 devices: a whole 4x8x8 slice. The times are simulated.
512 devices in a mesh: row: 32 (over y, x_lo, core), col: 16 (over z, x_hi).
Axes of the slice: x: 4 (x_hi: 2, x_lo: 2; x = x_hi * 2 + x_lo), y: 8, z: 8, core: 2. Of those that a mesh axis runs over, the one named last changes fastest.
Arguments:
- vectors: bfloat16 [64, 65536], P(None, ('row', 'col')), may hold values from -6 to 6
- tiles: bfloat16 [32, 16, 20, 128, 128], P('row', 'col'), may hold values from -0.078125 to 0.078125
- tile_row: int32 [32, 16, 20], P('row', 'col'), may hold values from -1 to 15, as said below
- tile_col: int32 [32, 16, 20], P('row', 'col'), may hold values from -1 to 31, as said below
Outputs:
- first_degree: bfloat16 [64, 65536], P(None, ('row', 'col'))
- second_degree: float32 [64, 65536], P(None, ('row', 'col'))
Inputs may be any that keep to these rules, and one draw needn't show every extreme that they name: tile_row and tile_col are -1 in the same slots. Slots of a device form groups of 16 in order (slot s in group floor(s / 16)); the slots of the first group are never empty. Within a group, the live slots have distinct values of tile_row. `tile_col`: see tile_row.
All inputs are finite; a program needn't handle non-finite values.
Results may differ from a plain program's by a relative error of at most 0.0025.
Values may be sent and summed in bfloat16 or wider, within the bound.
A program may use at most 64 MiB of HBM per device.

v0:
```python
import jax
import jax.numpy as jnp
from jax import lax
from jax.sharding import PartitionSpec as P

CENTER = 0.5
HALF_WIDTH = 1.5


def shards(vectors, tiles, tile_row, tile_col):
    local_tiles = tiles[0, 0]
    slot_rows = tile_row[0, 0]
    slot_cols = tile_col[0, 0]
    count_vec = vectors.shape[0]
    width = vectors.shape[1]
    block = local_tiles.shape[-1]
    per_block = width // block
    n_col = lax.axis_size("col")
    n_row = lax.axis_size("row")
    row_blocks = n_col * per_block
    col_blocks = n_row * per_block
    pick_rows = (slot_rows[:, None] == lax.broadcasted_iota(jnp.int32, (1, row_blocks), 1)).astype(
        jnp.bfloat16
    )
    pick_cols = (slot_cols[:, None] == lax.broadcasted_iota(jnp.int32, (1, col_blocks), 1)).astype(
        jnp.bfloat16
    )
    place_rows = pick_rows.astype(jnp.float32)
    place_cols = pick_cols.astype(jnp.float32)

    def gathered_left(pick, gathered, blocks):
        return jnp.einsum(
            "kr,vrb->kvb",
            pick,
            gathered.reshape(count_vec, blocks, block),
            preferred_element_type=jnp.float32,
        ).astype(jnp.bfloat16)

    def direct_terms(rows_x):
        left_rows = gathered_left(pick_rows, rows_x, row_blocks)
        to_cols = jnp.einsum(
            "kva,kab->kvb", left_rows, local_tiles, preferred_element_type=jnp.float32
        )
        return jnp.einsum(
            "kc,kvb->vcb", place_cols, to_cols, precision=lax.Precision.HIGHEST
        ).reshape(count_vec, col_blocks * block)

    def apply_hamiltonian(current):
        cols_x = lax.all_gather(current, "row", axis=1, tiled=True)
        left_cols = gathered_left(pick_cols, cols_x, col_blocks)
        to_rows = jnp.einsum(
            "kvb,kab->kva", left_cols, local_tiles, preferred_element_type=jnp.float32
        )
        row_terms = jnp.einsum("kr,kva->vra", place_rows, to_rows, precision=lax.Precision.HIGHEST)
        rows_x = lax.all_gather(current, "col", axis=1, tiled=True)
        col_terms = direct_terms(rows_x)
        row_half = lax.psum_scatter(
            row_terms.reshape(count_vec, row_blocks * block), "col", scatter_dimension=1, tiled=True
        )
        column_half = lax.psum_scatter(col_terms, "row", scatter_dimension=1, tiled=True)
        return row_half + column_half

    hx = apply_hamiltonian(vectors)
    first = ((hx - CENTER * vectors.astype(jnp.float32)) / HALF_WIDTH).astype(jnp.bfloat16)
    hy = apply_hamiltonian(first)
    second = 2.0 * (hy - CENTER * first.astype(jnp.float32)) / HALF_WIDTH - vectors.astype(
        jnp.float32
    )
    return (first, second)


def solution(mesh):
    placed = (
        P(None, ("row", "col")),
        P("row", "col", None, None, None),
        P("row", "col", None),
        P("row", "col", None),
    )
    return jax.shard_map(
        shards,
        mesh=mesh,
        in_specs=placed,
        out_specs=(P(None, ("row", "col")), P(None, ("row", "col"))),
        check_vma=False,
    )
```

profile of v0, /device:TPU:1, one launch (start us, length us, event | category | flops | bytes accessed | tf_op | source)
XLA Modules:
  0.0 737.1 jit_solution(9082555154138092483)
XLA Ops:
  7.2 39.0 %all_gather.12 = bf16[64,4096]{1,0:T(8,128)(2,1)S(1)} all-gather(bf16[64,128]{1,0:T(8,128)(2,1)} %param.4), channel_id=1, replica_groups=mesh['row'=32,'col'=16] {'row'}, dimensions={1}, use_global_device_ids=true | all-gather | bytes 540672 | tf_op jit(solution)/shard_map/all_gather | solution.py:49
  46.2 0.1 copy.14
  46.3 0.6 copy-done.4
  46.9 0.3 fusion.24
  47.3 0.5 fusion.14
  47.8 0.7 copy-done.3
  48.5 0.8 fusion.6
  49.3 1.0 copy.45
  50.3 0.6 copy-done.1
  51.0 40.2 %all_gather.13 = bf16[64,2048]{1,0:T(8,128)(2,1)S(1)} all-gather(bf16[64,128]{1,0:T(8,128)(2,1)S(1)} %copy-done.1), channel_id=1, replica_groups=mesh['row'=32,'col'=16] {'col'}, dimensions={1}, use_global_device_ids=true | all-gather | bytes 278528 | tf_op jit(solution)/shard_map/all_gather | solution.py:55
  91.3 0.3 fusion.30
  91.6 0.3 fusion.12
  91.9 1.1 fusion.4
  93.0 1.6 copy.43
  94.6 0.0 reduce-scatter.9.cloned.1.call-start
  94.6 154.4 %reduce-scatter.5.cloned.1.call-done = f32[64,128]{1,0:T(8,128)} async-done(((f32[64,2048]{1,0:T(8,128)}), f32[64,128]{1,0:T(8,128)}) %reduce-scatter.5.cloned.1.call-update) | async-done | bytes 32784 | tf_op jit(solution)/shard_map/reduce_scatter | solution.py:57
  249.0 122.1 %reduce-scatter.7.cloned.1.call-done = f32[64,128]{1,0:T(8,128)} async-done(((f32[64,4096]{1,0:T(8,128)}), f32[64,128]{1,0:T(8,128)}) %reduce-scatter.7.cloned.1.call-update) | async-done | bytes 32784 | tf_op jit(solution)/shard_map/reduce_scatter | solution.py:60
  371.1 0.8 fusion.18
  371.9 34.9 %all_gather.14 = bf16[64,4096]{1,0:T(8,128)(2,1)S(1)} all-gather(bf16[64,128]{1,0:T(8,128)(2,1)S(1)} %fusion.18), channel_id=1, replica_groups=mesh['row'=32,'col'=16] {'row'}, dimensions={1}, use_global_device_ids=true | all-gather | bytes 540672 | tf_op jit(solution)/shard_map/all_gather | solution.py:49
  406.8 0.1 copy.18
  406.9 0.3 fusion.21
  407.2 0.5 fusion.10
  407.8 0.8 fusion.2
  408.6 1.0 copy.44
  409.7 36.4 %all_gather.15 = bf16[64,2048]{1,0:T(8,128)(2,1)S(1)} all-gather(bf16[64,128]{1,0:T(8,128)(2,1)S(1)} %fusion.18), channel_id=1, replica_groups=mesh['row'=32,'col'=16] {'col'}, dimensions={1}, use_global_device_ids=true | all-gather | bytes 278528 | tf_op jit(solution)/shard_map/all_gather | solution.py:55
  446.1 0.3 fusion.27
  446.4 0.3 fusion.8
  446.7 1.1 fusion
  447.8 1.6 copy.42
  449.4 157.8 %reduce-scatter.9.cloned.1.call-done = f32[64,128]{1,0:T(8,128)} async-done(((f32[64,2048]{1,0:T(8,128)}), f32[64,128]{1,0:T(8,128)}) %reduce-scatter.9.cloned.1.call-update) | async-done | bytes 32784 | tf_op jit(solution)/shard_map/reduce_scatter | solution.py:57
  607.2 121.9 %reduce-scatter.11.cloned.1.call-done = f32[64,128]{1,0:T(8,128)} async-done(((f32[64,4096]{1,0:T(8,128)}), f32[64,128]{1,0:T(8,128)}) %reduce-scatter.11.cloned.1.call-update) | async-done | bytes 32784 | tf_op jit(solution)/shard_map/reduce_scatter | solution.py:60
  729.1 1.4 convert_subtract_fusion
  (16 shorter events, 0.3 us)
Async XLA Ops:
  7.2 40.1 %copy-start = (bf16[1,1,20,128,128]{4,3,2,1,0:T(8,128)(2,1)S(1)}, bf16[1,1,20,128,128]{4,3,2,1,0:T(8,128)(2,1)}, u32[]{:S(2)}) copy-start(bf16[1,1,20,128,128]{4,3,2,1,0:T(8,128)(2,1)} %param.5) | copy-start | bytes 1966084
  7.2 241.8 %reduce-scatter.5.cloned.1.call-start = ((), (), s32[]{:S(2)}) async-start(), calls=%async_computation.4 | async-start | bytes 557056 | tf_op jit(solution)/shard_map/reduce_scatter | solution.py:57
  46.3 0.7 copy-start.4
  47.8 0.7 copy-start.3
  50.3 0.7 copy-start.1
  50.3 320.8 %reduce-scatter.7.cloned.1.call-start = ((), (), s32[]{:S(2)}) async-start(), calls=%async_computation.5 | async-start | bytes 1081344 | tf_op jit(solution)/shard_map/reduce_scatter | solution.py:60
  94.6 512.6 %reduce-scatter.9.cloned.1.call-start = ((), (), s32[]{:S(2)}) async-start(), calls=%async_computation.6 | async-start | bytes 557056 | tf_op jit(solution)/shard_map/reduce_scatter | solution.py:57
  371.9 357.2 %copy-start.2 = (bf16[64,128]{1,0:T(8,128)(2,1)}, bf16[64,128]{1,0:T(8,128)(2,1)S(1)}, u32[]{:S(2)}) copy-start(bf16[64,128]{1,0:T(8,128)(2,1)S(1)} %fusion.18) | copy-start | bytes 49156
  409.6 319.5 %reduce-scatter.11.cloned.1.call-start = ((), (), s32[]{:S(2)}) async-start(), calls=%async_computation.7 | async-start | bytes 1081344 | tf_op jit(solution)/shard_map/reduce_scatter | solution.py:60
Sparse Core Ops, SparseCore 0:
  50.4 198.5 reduce-scatter.4
  252.0 119.0 reduce-scatter.6
  409.7 197.4 reduce-scatter.8
  610.1 119.0 reduce-scatter.10
where the time goes:
time: 739 us; the launch traced here: 737 us
  waiting for transfers between devices  556 us (75%)
  blocking collectives  151 us (20%)
  between operations  13.9 us (2%)
    reduce_scatter x2, waiting for transfers between devices, apply_hamiltonian(): lax.psum_scatter(row_terms.reshape(count_vec, row_blocks * block), 'col',...  312 us
    reduce_scatter x2, waiting for transfers between devices, apply_hamiltonian(): lax.psum_scatter(col_terms, 'row', scatter_dimension=1, tiled=True)  244 us
    all_gather x2, blocking collectives, apply_hamiltonian(): rows_x = lax.all_gather(current, 'col', axis=1, tiled=True)  76.7 us
    all_gather x2, blocking collectives, apply_hamiltonian(): cols_x = lax.all_gather(current, 'row', axis=1, tiled=True)  73.9 us
  transfers between devices with their start and end apart: 4, of which 4 were waited for; matrix products, arithmetic and copies ran while one was open for 1% of the time, Pallas kernels for 0%

commit v1 on v0

v1 whole, which is shorter than its diff:
```python
import functools

import jax
import jax.numpy as jnp
from jax import lax
from jax.experimental import pallas as pl
from jax.experimental.pallas import tpu as pltpu
from jax.sharding import PartitionSpec as P

CENTER = 0.5
HALF_WIDTH = 1.5
MESH = pl.DeviceIdType.MESH


def filter_kernel(
    n_row,
    n_col,
    slots,
    trow,
    tcol,
    x_ref,
    tiles_hbm,
    first_ref,
    second_ref,
    tiles,
    y_ref,
    rowx0,
    rowx1,
    colx0,
    colx1,
    part_c,
    part_r,
    swap_out,
    swap_in,
    out_c,
    out_r,
    in_c,
    in_r,
    slot_of_row,
    extra_of_row,
    prev_slot,
    last_slot,
    tiles_sem,
    send_gr,
    recv_gr,
    send_gc,
    recv_gc,
    send_fw,
    recv_fw,
    send_sw,
    recv_sw,
    send_sc,
    recv_sc,
    send_sr,
    recv_sr,
):
    r = lax.axis_index("row")
    c = lax.axis_index("col")
    chips = n_row // 2
    m = r // 2
    core = r - 2 * m
    partner = r + 1 - 2 * core
    zero_slot = slots
    rowx = (rowx0, rowx1)
    colx = (colx0, colx1)

    def row_peer(k):
        return lax.rem(c + k, n_col)

    def row_source(k):
        return lax.rem(c + n_col - k, n_col)

    def col_peer(k):
        return 2 * lax.rem(m + k, chips) + core

    def col_source(k):
        return 2 * lax.rem(m + chips - k, chips) + core

    tiles_copy = pltpu.make_async_copy(tiles_hbm, tiles, tiles_sem)
    tiles_copy.start()

    barrier = pltpu.get_barrier_semaphore()

    def hello_row(k, _):
        pl.semaphore_signal(barrier, inc=1, device_id=(r, row_peer(k)), device_id_type=MESH)
        return 0

    def hello_col(k, _):
        pl.semaphore_signal(barrier, inc=1, device_id=(col_peer(k), c), device_id_type=MESH)
        return 0

    lax.fori_loop(1, n_col, hello_row, 0)
    lax.fori_loop(1, chips, hello_col, 0)
    pl.semaphore_signal(barrier, inc=1, device_id=(partner, c), device_id_type=MESH)
    pl.semaphore_wait(barrier, n_col - 1 + chips - 1 + 1)

    def remote(src, dst, send, recv, row, col):
        return pltpu.make_async_remote_copy(
            src_ref=src, dst_ref=dst, send_sem=send, recv_sem=recv, device_id=(row, col), device_id_type=MESH
        )

    def gather_row(a, src, k):
        return remote(src, rowx[a].at[c], send_gr.at[a, k], recv_gr.at[a, k], r, row_peer(k))

    def gather_col(a, src, k):
        return remote(src, colx[a].at[r], send_gc.at[a, k], recv_gc.at[a, k], col_peer(k), c)

    def forward(a, src, k):
        return remote(src, colx[a].at[col_source(k)], send_fw.at[a, k], recv_fw.at[a, k], partner, c)

    def swap(a):
        return remote(swap_out, swap_in.at[a], send_sw.at[a], recv_sw.at[a], partner, c)

    def scatter_col(a, k):
        return remote(
            out_c.at[lax.rem(m + k, chips)], in_c.at[a, k], send_sc.at[a, k], recv_sc.at[a, k], col_peer(k), c
        )

    def scatter_row(a, k):
        return remote(out_r.at[row_peer(k)], in_r.at[a, k], send_sr.at[a, k], recv_sr.at[a, k], r, row_peer(k))

    def tables():
        def rows(p, _):
            one = jnp.int32(0)
            for s in range(n_col):
                one = jnp.where(trow[s] == p, s, one)
            two = jnp.int32(zero_slot)
            for s in range(n_col, slots):
                two = jnp.where(trow[s] == p, s, two)
            slot_of_row[p] = one
            extra_of_row[p] = two
            return 0

        lax.fori_loop(0, n_col, rows, 0)
        for s in range(slots):
            here = jnp.int32(zero_slot)
            for t in range(s):
                here = jnp.where(tcol[t] == tcol[s], t, here)
            prev_slot[s] = here

        def cols(q, _):
            here = jnp.int32(zero_slot)
            for s in range(slots):
                here = jnp.where(tcol[s] == q, s, here)
            last_slot[q] = here
            return 0

        lax.fori_loop(0, n_row, cols, 0)

    def apply(a, src):
        def start_gather(k, _):
            gather_row(a, src, k).start()
            gather_col(a, src, k).start()
            return 0

        forward(a, src, 0).start()
        lax.fori_loop(1, n_col, start_gather, 0)
        rowx[a][c] = src[...]
        colx[a][r] = src[...]
        if a == 0:
            part_c[zero_slot] = jnp.zeros(part_c.shape[1:], part_c.dtype)
            part_r[zero_slot] = jnp.zeros(part_r.shape[1:], part_r.dtype)
            tables()
            tiles_copy.wait()

        def pass_on(k, _):
            gather_col(a, src, k).wait_recv()
            forward(a, colx[a].at[col_source(k)], k).start()
            return 0

        lax.fori_loop(1, chips, pass_on, 0)

        def wait_row(k, _):
            gather_row(a, src, k).wait_recv()
            return 0

        lax.fori_loop(1, n_col, wait_row, 0)

        for s in range(slots):
            left = rowx[a][jnp.maximum(trow[s], 0)]
            part_c[s] = jnp.dot(left, tiles[s], preferred_element_type=jnp.float32)
        for s in range(slots):
            part_c[s] = part_c[s] + part_c[prev_slot[s]]

        if a == 1:
            swap(0).wait_send()

        def fill_swap(k, _):
            swap_out[k] = part_c[last_slot[2 * k + 1 - core]]
            return 0

        lax.fori_loop(0, chips, fill_swap, 0)
        swap(a).start()

        def wait_forward(k, _):
            forward(a, src, k).wait_recv()
            return 0

        lax.fori_loop(0, chips, wait_forward, 0)

        for s in range(slots):
            left = colx[a][jnp.maximum(tcol[s], 0)]
            part_r[s] = lax.dot_general(
                left, tiles[s], (((1,), (1,)), ((), ())), preferred_element_type=jnp.float32
            )

        if a == 1:

            def sent(k, _):
                scatter_row(0, k).wait_send()
                scatter_col(0, k).wait_send()
                return 0

            lax.fori_loop(1, n_col, sent, 0)

        def fill_row(k, _):
            p = row_peer(k)
            out_r[p] = part_r[slot_of_row[p]] + part_r[extra_of_row[p]]

            @pl.when(k < n_col)
            def _():
                scatter_row(a, k).start()

            return 0

        lax.fori_loop(1, n_col + 1, fill_row, 0)
        swap(a).wait_recv()

        def fill_col(k, _):
            q = lax.rem(m + k, chips)
            out_c[q] = part_c[last_slot[2 * q + core]] + swap_in[a, q]

            @pl.when(k < chips)
            def _():
                scatter_col(a, k).start()

            return 0

        lax.fori_loop(1, chips + 1, fill_col, 0)

        def add(k, total):
            scatter_row(a, k).wait_recv()
            scatter_col(a, k).wait_recv()
            return total + (in_r[a, k] + in_c[a, k])

        return lax.fori_loop(1, n_col, add, out_r[c] + out_c[m])

    x = x_ref[...].astype(jnp.float32)
    hx = apply(0, x_ref)
    y_ref[...] = ((hx - CENTER * x) / HALF_WIDTH).astype(jnp.bfloat16)
    hy = apply(1, y_ref)
    y = y_ref[...]
    first_ref[...] = y
    second_ref[...] = 2.0 * (hy - CENTER * y.astype(jnp.float32)) / HALF_WIDTH - x

    swap(1).wait_send()

    def drain(k, _):
        gather_row(0, x_ref, k).wait_send()
        gather_col(0, x_ref, k).wait_send()
        gather_row(1, y_ref, k).wait_send()
        gather_col(1, y_ref, k).wait_send()
        scatter_row(1, k).wait_send()
        scatter_col(1, k).wait_send()
        return 0

    lax.fori_loop(1, n_col, drain, 0)

    def drain_forward(k, _):
        forward(0, x_ref, k).wait_send()
        forward(1, y_ref, k).wait_send()
        return 0

    lax.fori_loop(0, chips, drain_forward, 0)


def shards(vectors, tiles, tile_row, tile_col):
    n_row = lax.axis_size("row")
    n_col = lax.axis_size("col")
    slots = tiles.shape[2]
    block = tiles.shape[-1]
    count = vectors.shape[0]
    chips = n_row // 2
    f32, bf16 = jnp.float32, jnp.bfloat16
    dma = pltpu.SemaphoreType.DMA
    vmem = pl.BlockSpec(memory_space=pltpu.VMEM)
    smem = pl.BlockSpec(memory_space=pltpu.SMEM)
    return pl.pallas_call(
        functools.partial(filter_kernel, n_row, n_col, slots),
        out_shape=(
            jax.ShapeDtypeStruct((count, block), bf16),
            jax.ShapeDtypeStruct((count, block), f32),
        ),
        in_specs=[smem, smem, vmem, pl.BlockSpec(memory_space=pl.ANY)],
        out_specs=(vmem, vmem),
        scratch_shapes=[
            pltpu.VMEM((slots, block, block), bf16),
            pltpu.VMEM((count, block), bf16),
            pltpu.VMEM((n_col, count, block), bf16),
            pltpu.VMEM((n_col, count, block), bf16),
            pltpu.VMEM((n_row, count, block), bf16),
            pltpu.VMEM((n_row, count, block), bf16),
            pltpu.VMEM((slots + 1, count, block), f32),
            pltpu.VMEM((slots + 1, count, block), f32),
            pltpu.VMEM((chips, count, block), f32),
            pltpu.VMEM((2, chips, count, block), f32),
            pltpu.VMEM((chips, count, block), f32),
            pltpu.VMEM((n_col, count, block), f32),
            pltpu.VMEM((2, chips, count, block), f32),
            pltpu.VMEM((2, n_col, count, block), f32),
            pltpu.SMEM((n_col,), jnp.int32),
            pltpu.SMEM((n_col,), jnp.int32),
            pltpu.SMEM((slots,), jnp.int32),
            pltpu.SMEM((n_row,), jnp.int32),
            dma(()),
            dma((2, n_col)),
            dma((2, n_col)),
            dma((2, chips)),
            dma((2, chips)),
            dma((2, chips)),
            dma((2, chips)),
            dma((2,)),
            dma((2,)),
            dma((2, chips)),
            dma((2, chips)),
            dma((2, n_col)),
            dma((2, n_col)),
        ],
        compiler_params=pltpu.CompilerParams(
            collective_id=0, has_side_effects=True, vmem_limit_bytes=32 * 1024 * 1024
        ),
        cost_estimate=pl.CostEstimate(
            flops=8 * slots * count * block * block, bytes_accessed=2 * slots * block * block, transcendentals=0
        ),
    )(tile_row[0, 0], tile_col[0, 0], vectors, tiles[0, 0])


def solution(mesh):
    placed = (
        P(None, ("row", "col")),
        P("row", "col", None, None, None),
        P("row", "col", None),
        P("row", "col", None),
    )
    return jax.shard_map(
        shards,
        mesh=mesh,
        in_specs=placed,
        out_specs=(P(None, ("row", "col")), P(None, ("row", "col"))),
        check_vma=False,
    )
```

time: 739 us -> 77.4 us (0.10)
  waiting for transfers between devices: 556 us -> 0 us
  blocking collectives: 151 us -> 0 us
  Pallas kernels: 0 us -> 72.8 us
  between operations: 13.9 us -> 0.66 us
    reduce_scatter x4 -> x0, waiting for transfers between devices: 556 us -> none  [the longest x2 312 us: apply_hamiltonian(): lax.psum_scatter(row_terms.reshape(count_vec, row_blocks * block), 'col',...]
    all_gather x4 -> x0, blocking collectives: 151 us -> none  [the longest x2 76.7 us: apply_hamiltonian(): rows_x = lax.all_gather(current, 'col', axis=1, tiled=True)]
    pallas_call x0 -> x1, Pallas kernels: none -> 72.8 us  [shards(): pl.pallas_call(functools.partial(filter_kernel, n_row, n_col, slots), out...]
  transfers between devices with their start and end apart: 4 -> 0, of which waited for: 4 -> 0; matrix products, arithmetic and copies ran while one was open for 1% -> 0% of each run, Pallas kernels for 0% -> 0%
where the time goes in v1:
time: 77.4 us; the launch traced here: 77.1 us
  Pallas kernels  72.8 us (94%)
  local copies, waits for them, and re-layouts  3.68 us (5%)
    pallas_call x1, Pallas kernels, shards(): pl.pallas_call(functools.partial(filter_kernel, n_row, n_col, slots), out...  72.8 us
    unnamed x10, local copies, waits for them, and re-layouts  3.68 us

profile of v1, /device:TPU:1, one launch (start us, length us, event | category | flops | bytes accessed | tf_op | source)
XLA Modules:
  0.0 77.1 jit_solution(17004032866864819413)
XLA Ops:
  0.6 0.0 copy-start.2
  0.6 0.0 copy-start.3
  0.7 0.6 copy-done.2
  1.3 0.0 copy-done.3
  1.3 0.0 copy-start
  1.3 1.1 %copy-done = bf16[1,1,20,128,128]{4,3,2,1,0:T(8,128)(2,1)S(1)} copy-done((bf16[1,1,20,128,128]{4,3,2,1,0:T(8,128)(2,1)S(1)}, bf16[1,1,20,128,128]{4,3,2,1,0:T(8,128)(2,1)}, u32[]{:S(2)}) %copy-start) | copy-done | bytes 655384
  2.4 0.0 copy-start.1
  2.4 0.7 copy-done.1
  3.1 72.8 %shard_map.59 = (bf16[64,128]{1,0:T(8,128)(2,1)S(1)}, f32[64,128]{1,0:T(8,128)S(1)}) custom-call(s32[20]{0:T(128)S(1)} %bitcast.4, s32[20]{0:T(128)S(1)} %bitcast.5, bf16[64,128]{1,0:T(8,128)(2,1)S(1)} %copy-done.1, bf16[20,128,128]{2,1,0:T(8,128)(2,1)S(1)} %bitcast.3), custom_call_target="tpu_custom_call" | custom-call | flops 167772160 | bytes 655360 | tf_op jit(solution)/shard_map/pallas_call | solution.py:288
  75.9 0.6 copy.8
  76.5 0.6 copy.9
Async XLA Ops:
  0.6 0.7 copy-start.2
  0.6 0.7 copy-start.3
  1.3 1.1 %copy-start = (bf16[1,1,20,128,128]{4,3,2,1,0:T(8,128)(2,1)S(1)}, bf16[1,1,20,128,128]{4,3,2,1,0:T(8,128)(2,1)}, u32[]{:S(2)}) copy-start(bf16[1,1,20,128,128]{4,3,2,1,0:T(8,128)(2,1)} %param.5) | copy-start | bytes 1966084
  2.4 0.7 copy-start.1

commit v2 on v0

v2 whole, which is shorter than its diff:
```python
import functools

import jax
import jax.numpy as jnp
from jax import lax
from jax.experimental import pallas as pl
from jax.experimental.pallas import tpu as pltpu
from jax.sharding import PartitionSpec as P

CENTER = 0.5
HALF_WIDTH = 1.5
MESH = pl.DeviceIdType.MESH
PARTS = 2

LIMITS = (2.0**12, 2.0**24)
TINY = 1e-30


def encode(v, limit):
    root = lax.rsqrt(lax.rsqrt(lax.rsqrt(lax.rsqrt(jnp.maximum(jnp.abs(v), TINY)))))
    code = root * (32767.0 / limit ** (1 / 16)) + 0.5
    code = jnp.where(jnp.abs(v) <= TINY, 0.0, code)
    return jnp.where(v < 0, -code, code).astype(jnp.int32).astype(jnp.int16)


def decode(code, limit):
    code = code.astype(jnp.int32).astype(jnp.float32)
    root = code * (limit ** (1 / 16) / 32767.0)
    power = root * root
    power = power * power
    power = power * power
    power = power * power
    return jnp.where(code < 0, -power, power)


def filter_kernel(n_row, n_col, slots, trow_hbm, tcol_hbm, x_hbm, tiles_hbm, first_ref, second_ref, *scratch):
    (
        trow_ref, tcol_ref, x_ref, tiles, y_ref, part_c, part_r, swap_out, swap_in, out_c, out_r, in_c, in_r,
        slot_of_row, extra_of_row, prev_slot, last_slot, fetch_sem,
        send_gr, recv_gr, send_gc, recv_gc, send_fw, recv_fw, send_sw, recv_sw, send_sc, recv_sc, send_sr, recv_sr,
    ) = scratch[:30]
    rowx = (scratch[30 : 30 + PARTS], scratch[30 + PARTS : 30 + 2 * PARTS])
    colx = (scratch[30 + 2 * PARTS : 30 + 3 * PARTS], scratch[30 + 3 * PARTS :])
    r = lax.axis_index("row")
    c = lax.axis_index("col")
    chips = n_row // 2
    assert chips == n_col
    ring = n_col // 2
    m = r // 2
    core = r - 2 * m
    partner = r + 1 - 2 * core
    zero_slot = slots
    height = x_ref.shape[0] // PARTS

    def offset(k):
        i = k // 2
        j = (i + 1) // 2
        return ring // 2 + j * (1 - 2 * (i % 2)), 1 - k % 2

    def peer(index, k):
        d, x = offset(k)
        return 2 * lax.rem(index // 2 + d, ring) + lax.rem(index % 2 + x, 2)

    def source(index, k):
        d, x = offset(k)
        return 2 * lax.rem(index // 2 + ring - d, ring) + lax.rem(index % 2 + x, 2)

    def row_peer(k):
        return peer(c, k)

    def col_peer(k):
        return 2 * peer(m, k) + core

    def col_source(k):
        return 2 * source(m, k) + core

    def fetch(i, src, dst):
        return pltpu.make_async_copy(src, dst, fetch_sem.at[i])

    fetch_x = fetch(0, x_hbm, x_ref)
    fetch_row = fetch(1, trow_hbm, trow_ref)
    fetch_col = fetch(2, tcol_hbm, tcol_ref)
    fetch_tiles = fetch(3, tiles_hbm, tiles)
    fetch_x.start()

    barrier = pltpu.get_barrier_semaphore()

    def hello(k, _):
        pl.semaphore_signal(barrier, inc=1, device_id=(r, row_peer(k)), device_id_type=MESH)
        pl.semaphore_signal(barrier, inc=1, device_id=(col_peer(k), c), device_id_type=MESH)
        return 0

    lax.fori_loop(0, n_col - 1, hello, 0)
    pl.semaphore_signal(barrier, inc=1, device_id=(partner, c), device_id_type=MESH)
    fetch_row.start()
    fetch_col.start()
    fetch_tiles.start()
    fetch_x.wait()
    pl.semaphore_wait(barrier, 2 * (n_col - 1) + 1)

    def remote(src, dst, send, recv, row, col):
        return pltpu.make_async_remote_copy(
            src_ref=src, dst_ref=dst, send_sem=send, recv_sem=recv, device_id=(row, col), device_id_type=MESH
        )

    def rows_of(h):
        return pl.ds(h * height, height)

    current = (x_ref, y_ref)

    def gather_row(a, h, k):
        src = current[a].at[rows_of(h)]
        return remote(src, rowx[a][h].at[c], send_gr.at[a, h, k], recv_gr.at[a, h, k], r, row_peer(k))

    def gather_col(a, h, k):
        src = current[a].at[rows_of(h)]
        return remote(src, colx[a][h].at[r], send_gc.at[a, h, k], recv_gc.at[a, h, k], col_peer(k), c)

    def forward(a, h, k):
        block = colx[a][h].at[col_source(k)]
        return remote(block, block, send_fw.at[a, h, k], recv_fw.at[a, h, k], partner, c)

    def swap(a, h):
        return remote(swap_out.at[a, h], swap_in.at[a, h], send_sw.at[a, h], recv_sw.at[a, h], partner, c)

    def scatter_col(a, h, k):
        return remote(
            out_c.at[a, h, k], in_c.at[a, h, k], send_sc.at[a, h, k], recv_sc.at[a, h, k], col_peer(k), c
        )

    def scatter_row(a, h, k):
        return remote(
            out_r.at[a, h, k], in_r.at[a, h, k], send_sr.at[a, h, k], recv_sr.at[a, h, k], r, row_peer(k)
        )

    def trow(s):
        return trow_ref[0, s]

    def tcol(s):
        return tcol_ref[0, s]

    def tables():
        part_c[zero_slot] = jnp.zeros(part_c.shape[1:], part_c.dtype)
        part_r[zero_slot] = jnp.zeros(part_r.shape[1:], part_r.dtype)

        def rows(p, _):
            one = jnp.int32(0)
            for s in range(n_col):
                one = jnp.where(trow(s) == p, s, one)
            two = jnp.int32(zero_slot)
            for s in range(n_col, slots):
                two = jnp.where(trow(s) == p, s, two)
            slot_of_row[p] = one
            extra_of_row[p] = two
            return 0

        lax.fori_loop(0, n_col, rows, 0)
        for s in range(slots):
            here = jnp.int32(zero_slot)
            for t in range(s):
                here = jnp.where(tcol(t) == tcol(s), t, here)
            prev_slot[s] = here

        def cols(q, _):
            here = jnp.int32(zero_slot)
            for s in range(slots):
                here = jnp.where(tcol(s) == q, s, here)
            last_slot[q] = here
            return 0

        lax.fori_loop(0, n_row, cols, 0)

    def start_gather(a, h):
        def start(k, _):
            gather_row(a, h, k).start()
            gather_col(a, h, k).start()
            return 0

        lax.fori_loop(0, n_col - 1, start, 0)
        block = current[a][rows_of(h)]
        rowx[a][h][c] = block
        colx[a][h][r] = block
        forward(a, h, n_col - 1).start()

    def products(a, h):
        def pass_on(k, _):
            gather_col(a, h, k).wait_recv()
            forward(a, h, k).start()
            return 0

        lax.fori_loop(0, chips - 1, pass_on, 0)

        def wait_row(k, _):
            gather_row(a, h, k).wait_recv()
            return 0

        lax.fori_loop(0, n_col - 1, wait_row, 0)
        for s in range(slots):
            left = rowx[a][h][jnp.maximum(trow(s), 0)]
            part_c[s] = jnp.dot(left, tiles[s], preferred_element_type=jnp.float32)
        for s in range(slots):
            part_c[s] = part_c[s] + part_c[prev_slot[s]]

        def fill_swap(k, _):
            swap_out[a, h, k] = part_c[last_slot[2 * k + 1 - core]]
            return 0

        lax.fori_loop(0, chips, fill_swap, 0)
        swap(a, h).start()

        def wait_forward(k, _):
            forward(a, h, k).wait_recv()
            return 0

        lax.fori_loop(0, chips, wait_forward, 0)
        for s in range(slots):
            left = colx[a][h][jnp.maximum(tcol(s), 0)]
            part_r[s] = lax.dot_general(
                left, tiles[s], (((1,), (1,)), ((), ())), preferred_element_type=jnp.float32
            )

        def row_sum(p):
            return part_r[slot_of_row[p]] + part_r[extra_of_row[p]]

        def col_sum(q):
            return part_c[last_slot[2 * q + core]] + swap_in[a, h, q]

        def send_row(k, _):
            out_r[a, h, k] = encode(row_sum(row_peer(k)), LIMITS[a])
            scatter_row(a, h, k).start()
            return 0

        lax.fori_loop(0, n_col - 1, send_row, 0)
        swap(a, h).wait_recv()

        def send_col(k, _):
            out_c[a, h, k] = encode(col_sum(peer(m, k)), LIMITS[a])
            scatter_col(a, h, k).start()
            return 0

        lax.fori_loop(0, chips - 1, send_col, 0)
        return row_sum(c) + col_sum(m)

    def collect(a, h, total):
        def add(k, total):
            scatter_row(a, h, k).wait_recv()
            scatter_col(a, h, k).wait_recv()
            return total + (decode(in_r[a, h, k], LIMITS[a]) + decode(in_c[a, h, k], LIMITS[a]))

        return lax.fori_loop(0, n_col - 1, add, total)

    parts = range(PARTS)
    for h in parts:
        start_gather(0, h)
    fetch_row.wait()
    fetch_col.wait()
    tables()
    fetch_tiles.wait()
    own = [products(0, h) for h in parts]
    for h in parts:
        hx = collect(0, h, own[h])
        x = x_ref[rows_of(h)].astype(jnp.float32)
        y_ref[rows_of(h)] = ((hx - CENTER * x) / HALF_WIDTH).astype(jnp.bfloat16)
        start_gather(1, h)
    own = [products(1, h) for h in parts]
    for h in parts:
        hy = collect(1, h, own[h])
        x = x_ref[rows_of(h)].astype(jnp.float32)
        y = y_ref[rows_of(h)]
        first_ref[rows_of(h)] = y
        second_ref[rows_of(h)] = 2.0 * (hy - CENTER * y.astype(jnp.float32)) / HALF_WIDTH - x

    for a in range(2):
        for h in parts:
            swap(a, h).wait_send()
            forward(a, h, n_col - 1).wait_send()

            def drain(k, _):
                gather_row(a, h, k).wait_send()
                gather_col(a, h, k).wait_send()
                forward(a, h, k).wait_send()
                scatter_row(a, h, k).wait_send()
                scatter_col(a, h, k).wait_send()
                return 0

            lax.fori_loop(0, n_col - 1, drain, 0)


def shards(vectors, tiles, tile_row, tile_col):
    n_row = lax.axis_size("row")
    n_col = lax.axis_size("col")
    slots = tiles.shape[2]
    block = tiles.shape[-1]
    count = vectors.shape[0]
    chips = n_row // 2
    height = count // PARTS
    f32, bf16, i16 = jnp.float32, jnp.bfloat16, jnp.int16
    dma = pltpu.SemaphoreType.DMA
    vmem = pl.BlockSpec(memory_space=pltpu.VMEM)
    hbm = pl.BlockSpec(memory_space=pltpu.HBM)
    return pl.pallas_call(
        functools.partial(filter_kernel, n_row, n_col, slots),
        out_shape=(
            jax.ShapeDtypeStruct((count, block), bf16),
            jax.ShapeDtypeStruct((count, block), f32),
        ),
        in_specs=[hbm] * 4,
        out_specs=(vmem, vmem),
        scratch_shapes=[
            pltpu.SMEM((1, slots), jnp.int32),
            pltpu.SMEM((1, slots), jnp.int32),
            pltpu.VMEM((count, block), bf16),
            pltpu.VMEM((slots, block, block), bf16),
            pltpu.VMEM((count, block), bf16),
            pltpu.VMEM((slots + 1, height, block), f32),
            pltpu.VMEM((slots + 1, height, block), f32),
            pltpu.VMEM((2, PARTS, chips, height, block), f32),
            pltpu.VMEM((2, PARTS, chips, height, block), f32),
            pltpu.VMEM((2, PARTS, chips, height, block), i16),
            pltpu.VMEM((2, PARTS, n_col, height, block), i16),
            pltpu.VMEM((2, PARTS, chips, height, block), i16),
            pltpu.VMEM((2, PARTS, n_col, height, block), i16),
            pltpu.SMEM((n_col,), jnp.int32),
            pltpu.SMEM((n_col,), jnp.int32),
            pltpu.SMEM((slots,), jnp.int32),
            pltpu.SMEM((n_row,), jnp.int32),
            dma((4,)),
        ]
        + [dma((2, PARTS, n_col))] * 6
        + [dma((2, PARTS))] * 2
        + [dma((2, PARTS, n_col))] * 4
        + [pltpu.VMEM((n_col, height, block), bf16)] * (2 * PARTS)
        + [pltpu.VMEM((n_row, height, block), bf16)] * (2 * PARTS),
        compiler_params=pltpu.CompilerParams(
            collective_id=0, has_side_effects=True, vmem_limit_bytes=48 * 1024 * 1024
        ),
        cost_estimate=pl.CostEstimate(
            flops=8 * slots * count * block * block, bytes_accessed=2 * slots * block * block, transcendentals=0
        ),
    )(tile_row[0], tile_col[0], vectors, tiles[0, 0])


def solution(mesh):
    placed = (
        P(None, ("row", "col")),
        P("row", "col", None, None, None),
        P("row", "col", None),
        P("row", "col", None),
    )
    return jax.shard_map(
        shards,
        mesh=mesh,
        in_specs=placed,
        out_specs=(P(None, ("row", "col")), P(None, ("row", "col"))),
        check_vma=False,
    )
```

time: 739 us -> 60.9 us (0.08)
  waiting for transfers between devices: 556 us -> 0 us
  blocking collectives: 151 us -> 0 us
  Pallas kernels: 0 us -> 56.3 us
  between operations: 13.9 us -> 0.66 us
    reduce_scatter x4 -> x0, waiting for transfers between devices: 556 us -> none  [the longest x2 312 us: apply_hamiltonian(): lax.psum_scatter(row_terms.reshape(count_vec, row_blocks * block), 'col',...]
    all_gather x4 -> x0, blocking collectives: 151 us -> none  [the longest x2 76.7 us: apply_hamiltonian(): rows_x = lax.all_gather(current, 'col', axis=1, tiled=True)]
    pallas_call x0 -> x1, Pallas kernels: none -> 56.3 us  [shards(): pl.pallas_call(functools.partial(filter_kernel, n_row, n_col, slots), out...]
  transfers between devices with their start and end apart: 4 -> 0, of which waited for: 4 -> 0; matrix products, arithmetic and copies ran while one was open for 1% -> 0% of each run, Pallas kernels for 0% -> 0%
where the time goes in v2:
time: 60.9 us; the launch traced here: 60.6 us
  Pallas kernels  56.3 us (92%)
  local copies, waits for them, and re-layouts  3.68 us (6%)
  between operations  0.66 us (1%)
    pallas_call x1, Pallas kernels, shards(): pl.pallas_call(functools.partial(filter_kernel, n_row, n_col, slots), out...  56.3 us
    unnamed x10, local copies, waits for them, and re-layouts  3.68 us

profile of v2, /device:TPU:1, one launch (start us, length us, event | category | flops | bytes accessed | tf_op | source)
XLA Modules:
  0.0 60.6 jit_solution(6575207629702445466)
XLA Ops:
  0.6 0.0 copy-start.2
  0.6 0.0 copy-start.3
  0.7 0.6 %copy-done.2 = s32[1,1,20]{2,1,0:T(1,128)S(1)} copy-done((s32[1,1,20]{2,1,0:T(1,128)S(1)}, s32[1,1,20]{2,1,0:T(1,128)}, u32[]{:S(2)}) %copy-start.2) | copy-done | bytes 104
  1.3 0.0 copy-done.3
  1.3 0.0 copy-start
  1.3 1.1 %copy-done = bf16[1,1,20,128,128]{4,3,2,1,0:T(8,128)(2,1)S(1)} copy-done((bf16[1,1,20,128,128]{4,3,2,1,0:T(8,128)(2,1)S(1)}, bf16[1,1,20,128,128]{4,3,2,1,0:T(8,128)(2,1)}, u32[]{:S(2)}) %copy-start) | copy-done | bytes 655384
  2.4 0.0 copy-start.1
  2.4 0.7 %copy-done.1 = bf16[64,128]{1,0:T(8,128)(2,1)S(1)} copy-done((bf16[64,128]{1,0:T(8,128)(2,1)S(1)}, bf16[64,128]{1,0:T(8,128)(2,1)}, u32[]{:S(2)}) %copy-start.1) | copy-done | bytes 16408
  3.1 56.3 %shard_map.59 = (bf16[64,128]{1,0:T(8,128)(2,1)S(1)}, f32[64,128]{1,0:T(8,128)S(1)}) custom-call(s32[1,20]{1,0:T(1,128)S(1)} %bitcast.4, s32[1,20]{1,0:T(1,128)S(1)} %bitcast.5, bf16[64,128]{1,0:T(8,128)(2,1)S(1)} %copy-done.1, bf16[20,128,128]{2,1,0:T(8,128)(2,1)S(1)} %bitcast.3), custom_call_target="tpu_custom_call" | custom-call | flops 167772160 | bytes 655360 | tf_op jit(solution)/shard_map/pallas_call | solution.py:301
  59.4 0.6 %copy.8 = bf16[64,128]{1,0:T(8,128)(2,1)} copy(bf16[64,128]{1,0:T(8,128)(2,1)S(1)} %get-tuple-element.4) | data formatting | bytes 32768
  60.0 0.6 %copy.9 = f32[64,128]{1,0:T(8,128)} copy(f32[64,128]{1,0:T(8,128)S(1)} %get-tuple-element.5) | data formatting | bytes 65536
Async XLA Ops:
  0.6 0.7 %copy-start.2 = (s32[1,1,20]{2,1,0:T(1,128)S(1)}, s32[1,1,20]{2,1,0:T(1,128)}, u32[]{:S(2)}) copy-start(s32[1,1,20]{2,1,0:T(1,128)} %param.6) | copy-start | bytes 244
  0.6 0.7 %copy-start.3 = (s32[1,1,20]{2,1,0:T(1,128)S(1)}, s32[1,1,20]{2,1,0:T(1,128)}, u32[]{:S(2)}) copy-start(s32[1,1,20]{2,1,0:T(1,128)} %param.7) | copy-start | bytes 244
  1.3 1.1 %copy-start = (bf16[1,1,20,128,128]{4,3,2,1,0:T(8,128)(2,1)S(1)}, bf16[1,1,20,128,128]{4,3,2,1,0:T(8,128)(2,1)}, u32[]{:S(2)}) copy-start(bf16[1,1,20,128,128]{4,3,2,1,0:T(8,128)(2,1)} %param.5) | copy-start | bytes 1966084
  2.4 0.7 %copy-start.1 = (bf16[64,128]{1,0:T(8,128)(2,1)S(1)}, bf16[64,128]{1,0:T(8,128)(2,1)}, u32[]{:S(2)}) copy-start(bf16[64,128]{1,0:T(8,128)(2,1)} %x_hbm.1) | copy-start | bytes 49156

commit v3 on v2

v3 whole, which is shorter than its diff:
```python
import functools

import jax
import jax.numpy as jnp
from jax import lax
from jax.experimental import pallas as pl
from jax.experimental.pallas import tpu as pltpu
from jax.sharding import PartitionSpec as P

CENTER = 0.5
HALF_WIDTH = 1.5
MESH = pl.DeviceIdType.MESH
BATCH = 4
PARTS = 2

LIMITS = (2.0**12, 2.0**24)
SCALES = tuple(32767.0 / limit ** (1 / 16) for limit in LIMITS)
TINY = 1e-30
GROUP = 5


def encode(v, scale):
    root = lax.rsqrt(lax.rsqrt(lax.rsqrt(lax.rsqrt(jnp.maximum(jnp.abs(v), TINY)))))
    code = jnp.where(jnp.abs(v) <= TINY, 0.0, root * scale + 0.5)
    return jnp.where(v < 0, -code, code).astype(jnp.int32).astype(jnp.int16)


def decode(code, scale):
    code = code.astype(jnp.int32).astype(jnp.float32)
    power = code * scale
    power = power * power
    power = power * power
    power = power * power
    power = power * power
    return jnp.where(code < 0, -power, power)


def filter_kernel(n_row, n_col, slots, trow_hbm, tcol_hbm, x_hbm, tiles_hbm, first_ref, second_ref, *scratch):
    (
        trow_ref, tcol_ref, tiles, current, own, row_now, col_now, rowx, colx, part_c, part_r, swap_out, swap_in,
        out_c, out_r, in_c, in_r, slot_of_row, extra_of_row, prev_slot, last_slot, place_of_chip, row_place, col_place,
        fetch_sem, send_gr, recv_gr, send_gc, recv_gc, send_sc, recv_sc, send_sr, recv_sr,
        send_fw, recv_fw, send_sw, recv_sw,
    ) = scratch
    r = lax.axis_index("row")
    c = lax.axis_index("col")
    chips = n_row // 2
    assert chips == n_col
    ring = n_col // 2
    m = r // 2
    core = r - 2 * m
    partner = r + 1 - 2 * core
    zero_slot = slots
    height = current.shape[1] // PARTS
    peers = n_col - 1

    def loop(count, body, unroll=1):
        def step(k, _):
            body(k)
            return 0

        lax.fori_loop(0, count, step, 0, unroll=unroll)

    def offset(k):
        i = k // 2
        j = (i + 1) // 2
        return ring // 2 + j * (1 - 2 * (i % 2)), 1 - k % 2

    def peer(index, k):
        d, x = offset(k)
        return 2 * lax.rem(index // 2 + d, ring) + lax.rem(index % 2 + x, 2)

    def source(index, k):
        d, x = offset(k)
        return 2 * lax.rem(index // 2 + ring - d, ring) + lax.rem(index % 2 + x, 2)

    def row_peer(k):
        return peer(c, k)

    def col_peer(k):
        return 2 * peer(m, k) + core

    def fetch(i, src, dst):
        return pltpu.make_async_copy(src, dst, fetch_sem.at[i])

    fetch_x = fetch(0, x_hbm, current.at[0])
    fetch_row = fetch(1, trow_hbm, trow_ref)
    fetch_col = fetch(2, tcol_hbm, tcol_ref)
    fetch_tiles = fetch(3, tiles_hbm, tiles)
    fetch_x.start()

    barrier = pltpu.get_barrier_semaphore()

    @functools.partial(loop, peers)
    def _(k):
        pl.semaphore_signal(barrier, inc=1, device_id=(r, row_peer(k)), device_id_type=MESH)
        pl.semaphore_signal(barrier, inc=1, device_id=(col_peer(k), c), device_id_type=MESH)

    pl.semaphore_signal(barrier, inc=1, device_id=(partner, c), device_id_type=MESH)
    fetch_row.start()
    fetch_col.start()
    fetch_tiles.start()
    fetch_x.wait()
    pl.semaphore_wait(barrier, 2 * peers + 1)

    def remote(src, dst, send, recv, row, col):
        return pltpu.make_async_remote_copy(
            src_ref=src, dst_ref=dst, send_sem=send, recv_sem=recv, device_id=(row, col), device_id_type=MESH
        )

    def rows_of(h):
        return pl.ds(pl.multiple_of(h * height, height), height)

    def gather_row(a, h, k):
        src = current.at[a, rows_of(h)]
        return remote(src, rowx.at[a, h, k], send_gr.at[a, h, k], recv_gr.at[a, h, k], r, row_peer(k))

    def gather_col(a, h, k):
        src = current.at[a, rows_of(h)]
        dst = colx.at[a, h, core * chips + k]
        return remote(src, dst, send_gc.at[a, h, k], recv_gc.at[a, h, k], col_peer(k), c)

    def forward(a, h, j):
        blocks = colx.at[a, h, pl.ds(core * chips + j * BATCH, BATCH)]
        return remote(blocks, blocks, send_fw.at[a, h, j], recv_fw.at[a, h, j], partner, c)

    def swap(a, h, j):
        half = pl.ds(j * (chips // 2), chips // 2)
        return remote(
            swap_out.at[a, h, half], swap_in.at[a, h, half], send_sw.at[a, h, j], recv_sw.at[a, h, j], partner, c
        )

    def scatter_col(a, h, k):
        return remote(
            out_c.at[a, h, k], in_c.at[a, h, k], send_sc.at[a, h, k], recv_sc.at[a, h, k], col_peer(k), c
        )

    def scatter_row(a, h, k):
        return remote(
            out_r.at[a, h, k], in_r.at[a, h, k], send_sr.at[a, h, k], recv_sr.at[a, h, k], r, row_peer(k)
        )

    def trow(s):
        return trow_ref[0, s]

    def tcol(s):
        return tcol_ref[0, s]

    def tables():
        part_c[zero_slot] = jnp.zeros(part_c.shape[1:], part_c.dtype)
        part_r[zero_slot] = jnp.zeros(part_r.shape[1:], part_r.dtype)

        @functools.partial(loop, n_col)
        def _(p):
            one = jnp.int32(0)
            for s in range(n_col):
                one = jnp.where(trow(s) == p, s, one)
            two = jnp.int32(zero_slot)
            for s in range(n_col, slots):
                two = jnp.where(trow(s) == p, s, two)
            slot_of_row[p] = one
            extra_of_row[p] = two

        @functools.partial(loop, n_row)
        def _(q):
            here = jnp.int32(zero_slot)
            for s in range(slots):
                here = jnp.where(tcol(s) == q, s, here)
            last_slot[q] = here

        @functools.partial(loop, chips)
        def _(k):
            place_of_chip[source(m, k)] = k
            row_place[source(c, k)] = k

        @functools.partial(loop, slots)
        def _(s):
            here = jnp.int32(zero_slot)
            for t in range(slots):
                here = jnp.where((tcol(t) == tcol(s)) & (t < s), t, here)
            prev_slot[s] = here
            q = jnp.maximum(tcol(s), 0)
            col_place[s] = lax.rem(q, 2) * chips + place_of_chip[lax.div(q, 2)]

    def start_gather(a, h):
        @functools.partial(loop, peers)
        def _(k):
            gather_row(a, h, k).start()
            gather_col(a, h, k).start()

        block = current[a, rows_of(h)]
        rowx[a, h, n_col - 1] = block
        colx[a, h, core * chips + chips - 1] = block

    def products(a, h):
        scale = jnp.where(a == 0, SCALES[0], SCALES[1])

        @functools.partial(loop, chips // BATCH)
        def _(j):
            @functools.partial(loop, BATCH, unroll=True)
            def _(i):
                @pl.when(j * BATCH + i < peers)
                def _():
                    gather_col(a, h, j * BATCH + i).wait_recv()

            forward(a, h, j).start()

        @functools.partial(loop, peers, unroll=True)
        def _(k):
            gather_row(a, h, k).wait_recv()

        for k in range(n_col):
            row_now[k] = rowx[a, h, k]
        for s in range(slots):
            left = row_now[row_place[jnp.maximum(trow(s), 0)]]
            part_c[s] = jnp.dot(left, tiles[s], preferred_element_type=jnp.float32)
        for s in range(slots):
            part_c[s] = part_c[s] + part_c[prev_slot[s]]

        @functools.partial(loop, 2)
        def _(j):
            for i in range(chips // 2):
                k = j * (chips // 2) + i
                swap_out[a, h, k] = part_c[last_slot[2 * peer(m, k) + 1 - core]]

            swap(a, h, j).start()

        @functools.partial(loop, chips // BATCH)
        def _(j):
            forward(a, h, j).wait_recv()

        for k in range(n_row):
            col_now[k] = colx[a, h, k]
        for s in range(slots):
            part_r[s] = lax.dot_general(
                col_now[col_place[s]], tiles[s], (((1,), (1,)), ((), ())), preferred_element_type=jnp.float32
            )

        def row_sum(k):
            p = peer(c, k)
            return part_r[slot_of_row[p]] + part_r[extra_of_row[p]]

        def col_sum(k):
            return part_c[last_slot[2 * peer(m, k) + core]] + swap_in[a, h, k]

        def send(sums, out, copy):
            @functools.partial(loop, peers // GROUP)
            def _(g):
                for i in range(GROUP):
                    out[a, h, g * GROUP + i] = encode(sums(g * GROUP + i), scale)
                for i in range(GROUP):
                    copy(a, h, g * GROUP + i).start()

        send(row_sum, out_r, scatter_row)
        swap(a, h, 0).wait_recv()
        swap(a, h, 1).wait_recv()
        send(col_sum, out_c, scatter_col)
        own[h] = row_sum(n_col - 1) + col_sum(chips - 1)

    def collect(a, h):
        scale = jnp.where(a == 0, 1.0 / SCALES[0], 1.0 / SCALES[1])

        def add(g, total):
            for i in range(GROUP):
                scatter_row(a, h, g * GROUP + i).wait_recv()
                scatter_col(a, h, g * GROUP + i).wait_recv()
            for i in range(GROUP):
                k = g * GROUP + i
                total = total + (decode(in_r[a, h, k], scale) + decode(in_c[a, h, k], scale))
            return total

        return lax.fori_loop(0, peers // GROUP, add, own[h])

    @functools.partial(loop, 3)
    def _(a):
        @functools.partial(loop, PARTS)
        def _(h):
            @pl.when(a > 0)
            def _():
                total = collect(a - 1, h)
                before = current[a - 1, rows_of(h)].astype(jnp.float32)

                @pl.when(a == 1)
                def _():
                    first = ((total - CENTER * before) / HALF_WIDTH).astype(jnp.bfloat16)
                    current[1, rows_of(h)] = first
                    first_ref[rows_of(h)] = first

                @pl.when(a == 2)
                def _():
                    x = current[0, rows_of(h)].astype(jnp.float32)
                    second_ref[rows_of(h)] = 2.0 * (total - CENTER * before) / HALF_WIDTH - x

            @pl.when(a < 2)
            def _():
                start_gather(a, h)

        @pl.when(a == 0)
        def _():
            fetch_row.wait()
            fetch_col.wait()
            tables()
            fetch_tiles.wait()

        @pl.when(a < 2)
        def _():
            @functools.partial(loop, PARTS)
            def _(h):
                products(a, h)

    @functools.partial(loop, 2)
    def _(a):
        @functools.partial(loop, PARTS)
        def _(h):
            @functools.partial(loop, 2)
            def _(j):
                swap(a, h, j).wait_send()

            @functools.partial(loop, chips // BATCH)
            def _(j):
                forward(a, h, j).wait_send()

            @functools.partial(loop, peers)
            def _(k):
                gather_row(a, h, k).wait_send()
                gather_col(a, h, k).wait_send()
                scatter_row(a, h, k).wait_send()
                scatter_col(a, h, k).wait_send()


def shards(vectors, tiles, tile_row, tile_col):
    n_row = lax.axis_size("row")
    n_col = lax.axis_size("col")
    slots = tiles.shape[2]
    block = tiles.shape[-1]
    count = vectors.shape[0]
    chips = n_row // 2
    height = count // PARTS
    f32, bf16, i16 = jnp.float32, jnp.bfloat16, jnp.int16
    dma = pltpu.SemaphoreType.DMA
    vmem = pl.BlockSpec(memory_space=pltpu.VMEM)
    hbm = pl.BlockSpec(memory_space=pltpu.HBM)
    return pl.pallas_call(
        functools.partial(filter_kernel, n_row, n_col, slots),
        out_shape=(
            jax.ShapeDtypeStruct((count, block), bf16),
            jax.ShapeDtypeStruct((count, block), f32),
        ),
        in_specs=[hbm] * 4,
        out_specs=(vmem, vmem),
        scratch_shapes=[
            pltpu.SMEM((1, slots), jnp.int32),
            pltpu.SMEM((1, slots), jnp.int32),
            pltpu.VMEM((slots, block, block), bf16),
            pltpu.VMEM((2, count, block), bf16),
            pltpu.VMEM((PARTS, height, block), f32),
            pltpu.VMEM((n_col, height, block), bf16),
            pltpu.VMEM((n_row, height, block), bf16),
            pltpu.VMEM((2, PARTS, n_col, height, block), bf16),
            pltpu.VMEM((2, PARTS, n_row, height, block), bf16),
            pltpu.VMEM((slots + 1, height, block), f32),
            pltpu.VMEM((slots + 1, height, block), f32),
            pltpu.VMEM((2, PARTS, chips, height, block), f32),
            pltpu.VMEM((2, PARTS, chips, height, block), f32),
        ]
        + [pltpu.VMEM((2, PARTS, chips, height, block), i16)] * 4
        + [
            pltpu.SMEM((n_col,), jnp.int32),
            pltpu.SMEM((n_col,), jnp.int32),
            pltpu.SMEM((slots,), jnp.int32),
            pltpu.SMEM((n_row,), jnp.int32),
            pltpu.SMEM((chips,), jnp.int32),
            pltpu.SMEM((n_col,), jnp.int32),
            pltpu.SMEM((slots,), jnp.int32),
            dma((4,)),
        ]
        + [dma((2, PARTS, n_col))] * 8
        + [dma((2, PARTS, chips // BATCH))] * 2
        + [dma((2, PARTS, 2))] * 2,
        compiler_params=pltpu.CompilerParams(
            collective_id=0, has_side_effects=True, vmem_limit_bytes=64 * 1024 * 1024 - 4096
        ),
        cost_estimate=pl.CostEstimate(
            flops=8 * slots * count * block * block, bytes_accessed=2 * slots * block * block, transcendentals=0
        ),
    )(tile_row[0], tile_col[0], vectors, tiles[0, 0])


def solution(mesh):
    placed = (
        P(None, ("row", "col")),
        P("row", "col", None, None, None),
        P("row", "col", None),
        P("row", "col", None),
    )
    return jax.shard_map(
        shards,
        mesh=mesh,
        in_specs=placed,
        out_specs=(P(None, ("row", "col")), P(None, ("row", "col"))),
        check_vma=False,
    )
```

time: 60.9 us -> 58.2 us (0.956)
  local copies, waits for them, and re-layouts: 3.68 us -> 1.95 us
  Pallas kernels: 56.3 us -> 55.4 us
    unnamed x10 -> x4, local copies, waits for them, and re-layouts: 3.68 us -> 1.95 us
    pallas_call x1, Pallas kernels: 56.3 us -> 55.4 us  [shards(): pl.pallas_call(functools.partial(filter_kernel, n_row, n_col, slots), out...]
where the time goes in v3:
time: 58.2 us; the launch traced here: 58 us
  Pallas kernels  55.4 us (95%)
  local copies, waits for them, and re-layouts  1.95 us (3%)
  between operations  0.65 us (1%)
    pallas_call x1, Pallas kernels, shards(): pl.pallas_call(functools.partial(filter_kernel, n_row, n_col, slots), out...  55.4 us
    unnamed x4, local copies, waits for them, and re-layouts  1.95 us

profile of v3, /device:TPU:1, one launch (start us, length us, event | category | flops | bytes accessed | tf_op | source)
XLA Modules:
  0.0 58.0 jit_solution(13480576353715769975)
XLA Ops:
  0.6 55.4 %shard_map.59 = (bf16[64,128]{1,0:T(8,128)(2,1)}, f32[64,128]{1,0:T(8,128)}) custom-call(s32[1,20]{1,0:T(1,128)} %bitcast.4, s32[1,20]{1,0:T(1,128)} %bitcast.5, bf16[64,128]{1,0:T(8,128)(2,1)} %x_hbm.1, bf16[20,128,128]{2,1,0:T(8,128)(2,1)} %bitcast.3), custom_call_target="tpu_custom_call" | custom-call | flops 167772160 | bytes 655360 | tf_op jit(solution)/shard_map/pallas_call | solution.py:343
  56.1 0.0 copy-start
  56.1 1.3 %copy.8 = bf16[64,128]{1,0:T(8,128)(2,1)} copy(bf16[64,128]{1,0:T(8,128)(2,1)} %get-tuple-element.4) | data formatting | bytes 32768
  57.4 0.0 copy-done
  57.4 0.6 %copy.9 = f32[64,128]{1,0:T(8,128)} copy(f32[64,128]{1,0:T(8,128)S(1)} %copy-done) | data formatting | bytes 65536
Async XLA Ops:
  56.1 1.3 %copy-start = (f32[64,128]{1,0:T(8,128)S(1)}, f32[64,128]{1,0:T(8,128)}, u32[]{:S(2)}) copy-start(f32[64,128]{1,0:T(8,128)} %get-tuple-element.5) | copy-start | bytes 98308

commit v4 on v3

--- a/solution.py
+++ b/solution.py
@@ -16,7 +16,7 @@
 LIMITS = (2.0**12, 2.0**24)
 SCALES = tuple(32767.0 / limit ** (1 / 16) for limit in LIMITS)
 TINY = 1e-30
-GROUP = 5
+GROUP = 3
 
 
 def encode(v, scale):
@@ -38,7 +38,8 @@
 def filter_kernel(n_row, n_col, slots, trow_hbm, tcol_hbm, x_hbm, tiles_hbm, first_ref, second_ref, *scratch):
     (
         trow_ref, tcol_ref, tiles, current, own, row_now, col_now, rowx, colx, part_c, part_r, swap_out, swap_in,
-        out_c, out_r, in_c, in_r, slot_of_row, extra_of_row, prev_slot, last_slot, place_of_chip, row_place, col_place,
+        out_c, out_r, in_c, in_r, row_slot, row_extra, prev_slot, own_last, other_last, place_of_chip, row_place,
+        left_row, col_place,
         fetch_sem, send_gr, recv_gr, send_gc, recv_gc, send_sc, recv_sc, send_sr, recv_sr,
         send_fw, recv_fw, send_sw, recv_sw,
     ) = scratch
@@ -91,7 +92,7 @@
 
     barrier = pltpu.get_barrier_semaphore()
 
-    @functools.partial(loop, peers)
+    @functools.partial(loop, peers, unroll=True)
     def _(k):
         pl.semaphore_signal(barrier, inc=1, device_id=(r, row_peer(k)), device_id_type=MESH)
         pl.semaphore_signal(barrier, inc=1, device_id=(col_peer(k), c), device_id_type=MESH)
@@ -151,22 +152,26 @@
         part_r[zero_slot] = jnp.zeros(part_r.shape[1:], part_r.dtype)
 
         @functools.partial(loop, n_col)
-        def _(p):
+        def _(k):
+            p = peer(c, k)
             one = jnp.int32(0)
             for s in range(n_col):
                 one = jnp.where(trow(s) == p, s, one)
             two = jnp.int32(zero_slot)
             for s in range(n_col, slots):
                 two = jnp.where(trow(s) == p, s, two)
-            slot_of_row[p] = one
-            extra_of_row[p] = two
-
-        @functools.partial(loop, n_row)
-        def _(q):
-            here = jnp.int32(zero_slot)
+            row_slot[k] = one
+            row_extra[k] = two
+
+        @functools.partial(loop, chips)
+        def _(k):
+            q = 2 * peer(m, k) + core
+            mine, other = jnp.int32(zero_slot), jnp.int32(zero_slot)
             for s in range(slots):
-                here = jnp.where(tcol(s) == q, s, here)
-            last_slot[q] = here
+                mine = jnp.where(tcol(s) == q, s, mine)
+                other = jnp.where(tcol(s) == q + 1 - 2 * core, s, other)
+            own_last[k] = mine
+            other_last[k] = other
 
         @functools.partial(loop, chips)
         def _(k):
@@ -179,11 +184,12 @@
             for t in range(slots):
                 here = jnp.where((tcol(t) == tcol(s)) & (t < s), t, here)
             prev_slot[s] = here
+            left_row[s] = row_place[jnp.maximum(trow(s), 0)]
             q = jnp.maximum(tcol(s), 0)
             col_place[s] = lax.rem(q, 2) * chips + place_of_chip[lax.div(q, 2)]
 
     def start_gather(a, h):
-        @functools.partial(loop, peers)
+        @functools.partial(loop, peers, unroll=True)
         def _(k):
             gather_row(a, h, k).start()
             gather_col(a, h, k).start()
@@ -195,38 +201,25 @@
     def products(a, h):
         scale = jnp.where(a == 0, SCALES[0], SCALES[1])
 
-        @functools.partial(loop, chips // BATCH)
-        def _(j):
-            @functools.partial(loop, BATCH, unroll=True)
-            def _(i):
-                @pl.when(j * BATCH + i < peers)
-                def _():
-                    gather_col(a, h, j * BATCH + i).wait_recv()
-
+        for j in range(chips // BATCH):
+            for k in range(j * BATCH, min((j + 1) * BATCH, peers)):
+                gather_col(a, h, k).wait_recv()
             forward(a, h, j).start()
-
-        @functools.partial(loop, peers, unroll=True)
-        def _(k):
+        for k in range(peers):
             gather_row(a, h, k).wait_recv()
 
         for k in range(n_col):
             row_now[k] = rowx[a, h, k]
         for s in range(slots):
-            left = row_now[row_place[jnp.maximum(trow(s), 0)]]
-            part_c[s] = jnp.dot(left, tiles[s], preferred_element_type=jnp.float32)
+            part_c[s] = jnp.dot(row_now[left_row[s]], tiles[s], preferred_element_type=jnp.float32)
         for s in range(slots):
             part_c[s] = part_c[s] + part_c[prev_slot[s]]
 
-        @functools.partial(loop, 2)
-        def _(j):
-            for i in range(chips // 2):
-                k = j * (chips // 2) + i
-                swap_out[a, h, k] = part_c[last_slot[2 * peer(m, k) + 1 - core]]
-
+        for j in range(2):
+            for k in range(j * (chips // 2), (j + 1) * (chips // 2)):
+                swap_out[a, h, k] = part_c[other_last[k]]
             swap(a, h, j).start()
-
-        @functools.partial(loop, chips // BATCH)
-        def _(j):
+        for j in range(chips // BATCH):
             forward(a, h, j).wait_recv()
 
         for k in range(n_row):
@@ -237,19 +230,17 @@
             )
 
         def row_sum(k):
-            p = peer(c, k)
-            return part_r[slot_of_row[p]] + part_r[extra_of_row[p]]
+            return part_r[row_slot[k]] + part_r[row_extra[k]]
 
         def col_sum(k):
-            return part_c[last_slot[2 * peer(m, k) + core]] + swap_in[a, h, k]
+            return part_c[own_last[k]] + swap_in[a, h, k]
 
         def send(sums, out, copy):
-            @functools.partial(loop, peers // GROUP)
-            def _(g):
-                for i in range(GROUP):
-                    out[a, h, g * GROUP + i] = encode(sums(g * GROUP + i), scale)
-                for i in range(GROUP):
-                    copy(a, h, g * GROUP + i).start()
+            for g in range(0, peers, GROUP):
+                for k in range(g, g + GROUP):
+                    out[a, h, k] = encode(sums(k), scale)
+                for k in range(g, g + GROUP):
+                    copy(a, h, k).start()
 
         send(row_sum, out_r, scatter_row)
         swap(a, h, 0).wait_recv()
@@ -260,19 +251,41 @@
     def collect(a, h):
         scale = jnp.where(a == 0, 1.0 / SCALES[0], 1.0 / SCALES[1])
 
-        def add(g, total):
-            for i in range(GROUP):
-                scatter_row(a, h, g * GROUP + i).wait_recv()
-                scatter_col(a, h, g * GROUP + i).wait_recv()
-            for i in range(GROUP):
-                k = g * GROUP + i
+        total = own[h]
+        for g in range(0, peers, GROUP):
+            for k in range(g, g + GROUP):
+                scatter_row(a, h, k).wait_recv()
+                scatter_col(a, h, k).wait_recv()
+            for k in range(g, g + GROUP):
                 total = total + (decode(in_r[a, h, k], scale) + decode(in_c[a, h, k], scale))
-            return total
-
-        return lax.fori_loop(0, peers // GROUP, add, own[h])
+        return total
+
+    def drain():
+        @functools.partial(loop, 2)
+        def _(a):
+            @functools.partial(loop, PARTS)
+            def _(h):
+                @functools.partial(loop, 2)
+                def _(j):
+                    swap(a, h, j).wait_send()
+
+                @functools.partial(loop, chips // BATCH)
+                def _(j):
+                    forward(a, h, j).wait_send()
+
+                @functools.partial(loop, peers, unroll=5)
+                def _(k):
+                    gather_row(a, h, k).wait_send()
+                    gather_col(a, h, k).wait_send()
+                    scatter_row(a, h, k).wait_send()
+                    scatter_col(a, h, k).wait_send()
 
     @functools.partial(loop, 3)
     def _(a):
+        @pl.when(a == 2)
+        def _():
+            drain()
+
         @functools.partial(loop, PARTS)
         def _(h):
             @pl.when(a > 0)
@@ -307,25 +320,6 @@
             @functools.partial(loop, PARTS)
             def _(h):
                 products(a, h)
-
-    @functools.partial(loop, 2)
-    def _(a):
-        @functools.partial(loop, PARTS)
-        def _(h):
-            @functools.partial(loop, 2)
-            def _(j):
-                swap(a, h, j).wait_send()
-
-            @functools.partial(loop, chips // BATCH)
-            def _(j):
-                forward(a, h, j).wait_send()
-
-            @functools.partial(loop, peers)
-            def _(k):
-                gather_row(a, h, k).wait_send()
-                gather_col(a, h, k).wait_send()
-                scatter_row(a, h, k).wait_send()
-                scatter_col(a, h, k).wait_send()
 
 
 def shards(vectors, tiles, tile_row, tile_col):
@@ -368,9 +362,11 @@
             pltpu.SMEM((n_col,), jnp.int32),
             pltpu.SMEM((n_col,), jnp.int32),
             pltpu.SMEM((slots,), jnp.int32),
-            pltpu.SMEM((n_row,), jnp.int32),
+            pltpu.SMEM((chips,), jnp.int32),
+            pltpu.SMEM((chips,), jnp.int32),
             pltpu.SMEM((chips,), jnp.int32),
             pltpu.SMEM((n_col,), jnp.int32),
+            pltpu.SMEM((slots,), jnp.int32),
             pltpu.SMEM((slots,), jnp.int32),
             dma((4,)),
         ]
@@ -378,7 +374,7 @@
         + [dma((2, PARTS, chips // BATCH))] * 2
         + [dma((2, PARTS, 2))] * 2,
         compiler_params=pltpu.CompilerParams(
-            collective_id=0, has_side_effects=True, vmem_limit_bytes=64 * 1024 * 1024 - 4096
+            collective_id=0, has_side_effects=True, vmem_limit_bytes=64 * 1024 * 1024 - 600 * 1024
         ),
         cost_estimate=pl.CostEstimate(
             flops=8 * slots * count * block * block, bytes_accessed=2 * slots * block * block, transcendentals=0

time: 58.2 us -> 57.4 us (0.986)
  Pallas kernels: 55.4 us -> 54.6 us
    pallas_call x1, Pallas kernels: 55.4 us -> 54.6 us  [shards(): pl.pallas_call(functools.partial(filter_kernel, n_row, n_col, slots), out...]
where the time goes in v4:
time: 57.4 us; the launch traced here: 57.2 us
  Pallas kernels  54.6 us (95%)
  local copies, waits for them, and re-layouts  1.95 us (3%)
  between operations  0.65 us (1%)
    pallas_call x1, Pallas kernels, shards(): pl.pallas_call(functools.partial(filter_kernel, n_row, n_col, slots), out...  54.6 us
    unnamed x4, local copies, waits for them, and re-layouts  1.95 us

profile of v4, /device:TPU:1, one launch (start us, length us, event | category | flops | bytes accessed | tf_op | source)
XLA Modules:
  0.0 57.2 jit_solution(16743363415708546706)
XLA Ops:
  0.6 54.6 %shard_map.59 = (bf16[64,128]{1,0:T(8,128)(2,1)}, f32[64,128]{1,0:T(8,128)}) custom-call(s32[1,20]{1,0:T(1,128)} %bitcast.4, s32[1,20]{1,0:T(1,128)} %bitcast.5, bf16[64,128]{1,0:T(8,128)(2,1)} %x_hbm.1, bf16[20,128,128]{2,1,0:T(8,128)(2,1)} %bitcast.3), custom_call_target="tpu_custom_call" | custom-call | flops 167772160 | bytes 655360 | tf_op jit(solution)/shard_map/pallas_call | solution.py:337
  55.2 0.0 copy-start
  55.2 1.3 %copy.8 = bf16[64,128]{1,0:T(8,128)(2,1)} copy(bf16[64,128]{1,0:T(8,128)(2,1)} %get-tuple-element.4) | data formatting | bytes 32768
  56.5 0.0 copy-done
  56.5 0.6 %copy.9 = f32[64,128]{1,0:T(8,128)} copy(f32[64,128]{1,0:T(8,128)S(1)} %copy-done) | data formatting | bytes 65536
Async XLA Ops:
  55.2 1.3 %copy-start = (f32[64,128]{1,0:T(8,128)S(1)}, f32[64,128]{1,0:T(8,128)}, u32[]{:S(2)}) copy-start(f32[64,128]{1,0:T(8,128)} %get-tuple-element.5) | copy-start | bytes 98308

commit v5 on v4

--- a/solution.py
+++ b/solution.py
@@ -337,8 +337,8 @@
     return pl.pallas_call(
         functools.partial(filter_kernel, n_row, n_col, slots),
         out_shape=(
-            jax.ShapeDtypeStruct((count, block), bf16),
-            jax.ShapeDtypeStruct((count, block), f32),
+            pltpu.VMEM((count, block), bf16),
+            pltpu.VMEM((count, block), f32),
         ),
         in_specs=[hbm] * 4,
         out_specs=(vmem, vmem),
@@ -374,7 +374,7 @@
         + [dma((2, PARTS, chips // BATCH))] * 2
         + [dma((2, PARTS, 2))] * 2,
         compiler_params=pltpu.CompilerParams(
-            collective_id=0, has_side_effects=True, vmem_limit_bytes=64 * 1024 * 1024 - 600 * 1024
+            collective_id=0, has_side_effects=True, vmem_limit_bytes=60 * 1024 * 1024
         ),
         cost_estimate=pl.CostEstimate(
             flops=8 * slots * count * block * block, bytes_accessed=2 * slots * block * block, transcendentals=0

time: 57.4 us -> 55.8 us (0.972)
  Pallas kernels: 54.6 us -> 53.8 us
  local copies, waits for them, and re-layouts: 1.95 us -> 1.22 us
    pallas_call x1, Pallas kernels: 54.6 us -> 53.8 us  [shards(): pl.pallas_call(functools.partial(filter_kernel, n_row, n_col, slots), out...]
    unnamed x4 -> x2, local copies, waits for them, and re-layouts: 1.95 us -> 1.22 us
where the time goes in v5:
time: 55.8 us; the launch traced here: 55.6 us
  Pallas kernels  53.8 us (96%)
  local copies, waits for them, and re-layouts  1.22 us (2%)
  between operations  0.64 us (1%)
    pallas_call x1, Pallas kernels, shards(): pl.pallas_call(functools.partial(filter_kernel, n_row, n_col, slots), out...  53.8 us
    unnamed x2, local copies, waits for them, and re-layouts  1.22 us

profile of v5, /device:TPU:1, one launch (start us, length us, event | category | flops | bytes accessed | tf_op | source)
XLA Modules:
  0.0 55.6 jit_solution(15216650972441317822)
XLA Ops:
  0.6 53.8 %shard_map.59 = (bf16[64,128]{1,0:T(8,128)(2,1)S(1)}, f32[64,128]{1,0:T(8,128)S(1)}) custom-call(s32[1,20]{1,0:T(1,128)} %bitcast.4, s32[1,20]{1,0:T(1,128)} %bitcast.5, bf16[64,128]{1,0:T(8,128)(2,1)} %x_hbm.1, bf16[20,128,128]{2,1,0:T(8,128)(2,1)} %bitcast.3), custom_call_target="tpu_custom_call" | custom-call | flops 167772160 | bytes 655360 | tf_op jit(solution)/shard_map/pallas_call | solution.py:337
  54.4 0.6 %copy.8 = bf16[64,128]{1,0:T(8,128)(2,1)} copy(bf16[64,128]{1,0:T(8,128)(2,1)S(1)} %get-tuple-element.2) | data formatting | bytes 32768
  55.0 0.6 %copy.9 = f32[64,128]{1,0:T(8,128)} copy(f32[64,128]{1,0:T(8,128)S(1)} %get-tuple-element.3) | data formatting | bytes 65536

commit v6 on v5

--- a/solution.py
+++ b/solution.py
@@ -219,11 +219,13 @@
             for k in range(j * (chips // 2), (j + 1) * (chips // 2)):
                 swap_out[a, h, k] = part_c[other_last[k]]
             swap(a, h, j).start()
+        for k in range(chips):
+            col_now[core * chips + k] = colx[a, h, core * chips + k]
         for j in range(chips // BATCH):
             forward(a, h, j).wait_recv()
 
-        for k in range(n_row):
-            col_now[k] = colx[a, h, k]
+        for k in range(chips):
+            col_now[(1 - core) * chips + k] = colx[a, h, (1 - core) * chips + k]
         for s in range(slots):
             part_r[s] = lax.dot_general(
                 col_now[col_place[s]], tiles[s], (((1,), (1,)), ((), ())), preferred_element_type=jnp.float32
@@ -235,17 +237,19 @@
         def col_sum(k):
             return part_c[own_last[k]] + swap_in[a, h, k]
 
-        def send(sums, out, copy):
+        def send(sums, out, copy, swapped):
             for g in range(0, peers, GROUP):
+                if swapped and g == 0:
+                    swap(a, h, 0).wait_recv()
+                if swapped and g < chips // 2 <= g + GROUP:
+                    swap(a, h, 1).wait_recv()
                 for k in range(g, g + GROUP):
                     out[a, h, k] = encode(sums(k), scale)
                 for k in range(g, g + GROUP):
                     copy(a, h, k).start()
 
-        send(row_sum, out_r, scatter_row)
-        swap(a, h, 0).wait_recv()
-        swap(a, h, 1).wait_recv()
-        send(col_sum, out_c, scatter_col)
+        send(row_sum, out_r, scatter_row, False)
+        send(col_sum, out_c, scatter_col, True)
         own[h] = row_sum(n_col - 1) + col_sum(chips - 1)
 
     def collect(a, h):

time: 55.8 us -> 55.3 us (level)
  no operation moved by 1% of the time
where the time goes in v6:
time: 55.3 us; the launch traced here: 55.2 us
  Pallas kernels  53.3 us (96%)
  local copies, waits for them, and re-layouts  1.22 us (2%)
  between operations  0.64 us (1%)
    pallas_call x1, Pallas kernels, shards(): pl.pallas_call(functools.partial(filter_kernel, n_row, n_col, slots), out...  53.3 us
    unnamed x2, local copies, waits for them, and re-layouts  1.22 us

profile of v6, /device:TPU:1, one launch (start us, length us, event | category | flops | bytes accessed | tf_op | source)
XLA Modules:
  0.0 55.2 jit_solution(3666774764973042605)
XLA Ops:
  0.6 53.3 %shard_map.59 = (bf16[64,128]{1,0:T(8,128)(2,1)S(1)}, f32[64,128]{1,0:T(8,128)S(1)}) custom-call(s32[1,20]{1,0:T(1,128)} %bitcast.4, s32[1,20]{1,0:T(1,128)} %bitcast.5, bf16[64,128]{1,0:T(8,128)(2,1)} %x_hbm.1, bf16[20,128,128]{2,1,0:T(8,128)(2,1)} %bitcast.3), custom_call_target="tpu_custom_call" | custom-call | flops 167772160 | bytes 655360 | tf_op jit(solution)/shard_map/pallas_call | solution.py:341
  53.9 0.6 %copy.8 = bf16[64,128]{1,0:T(8,128)(2,1)} copy(bf16[64,128]{1,0:T(8,128)(2,1)S(1)} %get-tuple-element.2) | data formatting | bytes 32768
  54.5 0.6 %copy.9 = f32[64,128]{1,0:T(8,128)} copy(f32[64,128]{1,0:T(8,128)S(1)} %get-tuple-element.3) | data formatting | bytes 65536
